TPU v7x, 128 devices: a whole 4x4x4 slice. The times are simulated.
128 devices in a mesh: rows: 32 (over z, y, core), cols: 4 (over x).
Axes of the slice: x: 4, y: 4, z: 4, core: 2. Of those that a mesh axis runs over, the one named last changes fastest.
Arguments:
- basis: float32 [64, 262144], P('cols', 'rows'), may hold values from -450 to 450
- blocks: bfloat16 [1024, 4, 256, 256], P('rows'), may hold values from -16 to 1, as said below
- far_cols: int32 [1024], P('rows'), may hold values from 0 to 1023, as said below
Outputs:
- basis_out: float32 [64, 262144], P('cols', 'rows')
- ritz: float32 [64, 64], P(None, 'cols')
Inputs may be any that keep to these rules, and one draw needn't show every extreme that they name: Off-diagonal entries are positive; each diagonal entry of a diagonal block is minus the sum of the other entries of its row over the four blocks, rounded to bfloat16. `far_cols`: the block rows of one device name at most 2 far columns among the block rows of any one device; the block rows of some device are named by exactly 2 block rows of every device.
All inputs are finite; a program needn't handle non-finite values.
Results may differ from a plain program's by a relative error of at most 0.0036.
Values may be sent and summed in bfloat16 or wider, within the bound.
No kernel may reach another device: no remote copies, remote signals or barrier semaphores. Data moves between devices by JAX's collectives and lax.ppermute only.
A program may use at most 128 MiB of HBM per device.

v0:
```python
import jax
import jax.numpy as jnp
from jax import lax
from jax.sharding import PartitionSpec as P

ITERS = 4


def with_halo(block, sides, width):
    for axis, dim in sides:
        count = lax.axis_size(axis)
        forward = [(i, i + 1) for i in range(count - 1)]
        forward.append((count - 1, 0))
        backward = [(target, source) for source, target in forward]
        low = lax.ppermute(
            lax.slice_in_dim(block, block.shape[dim] - width, None, axis=dim), axis, forward
        )
        high = lax.ppermute(lax.slice_in_dim(block, 0, width, axis=dim), axis, backward)
        block = jnp.concatenate([low, block, high], axis=dim)
    return block


def block_product(pieces, blocks, position):
    return jnp.einsum(
        "jbt,bst->jbs", pieces, blocks[:, position], preferred_element_type=jnp.float32
    )


def body(basis, blocks, far_cols):
    width = basis.shape[0]
    block_rows = blocks.shape[0]
    block_size = blocks.shape[2]
    row_devices = lax.axis_size("rows")
    total_states = block_rows * block_size * row_devices
    modes = width * lax.axis_size("cols")
    highest = lax.Precision.HIGHEST

    def apply_generator(iterate_bf):
        shaped = iterate_bf.reshape(width, block_rows, block_size)
        result = block_product(shaped, blocks, 0)
        empty = jnp.zeros((width, block_rows, block_size), jnp.bfloat16)
        piece = lax.all_gather(shaped, "rows", axis=1, tiled=True)
        inside = jnp.logical_and(far_cols >= 0, far_cols < piece.shape[1])
        taken = jnp.take(piece, jnp.clip(far_cols, 0, piece.shape[1] - 1), axis=1)
        remote = jnp.where(inside[None, :, None], taken, empty)
        extended = with_halo(shaped, (("rows", 1),), 1)
        result = result + block_product(extended[:, :-2], blocks, 1)
        result = result + block_product(extended[:, 2:], blocks, 2)
        result = result + block_product(remote, blocks, 3)
        return result.reshape(width, block_rows * block_size)

    iterate = basis
    for step in range(ITERS):
        iterate = iterate + 0.2 * apply_generator(iterate.astype(jnp.bfloat16))
    whole_iterate = lax.all_gather(iterate, "cols", axis=0, tiled=True)
    contract = (((1,), (1,)), ((), ()))
    gram_part = lax.dot_general(whole_iterate, iterate, contract, precision=highest)
    column_start = lax.axis_index("cols") * width
    gram_mine = lax.psum(gram_part, "rows")
    gram = lax.all_gather(gram_mine, "cols", axis=1, tiled=True) / total_states
    applied = apply_generator(iterate.astype(jnp.bfloat16))
    product_part = lax.dot_general(whole_iterate, applied, contract, precision=highest)
    product_mine = lax.psum(product_part, "rows")
    product = lax.all_gather(product_mine, "cols", axis=1, tiled=True) / total_states
    factor = jnp.linalg.cholesky(gram)
    identity_square = jnp.eye(modes, dtype=factor.dtype)
    inverse_factor = lax.linalg.triangular_solve(
        factor, identity_square, left_side=True, lower=True
    )
    own_rows = lax.dynamic_slice_in_dim(inverse_factor, column_start, width, 0)
    basis_out = jnp.dot(own_rows, whole_iterate, precision=highest)
    left_part = jnp.dot(inverse_factor, product, precision=highest)
    ritz_whole = jnp.dot(left_part, inverse_factor.T, precision=highest)
    ritz = lax.dynamic_slice_in_dim(ritz_whole, column_start, width, 1)
    return (basis_out, ritz)


def solution(mesh):
    in_specs = (P("cols", "rows"), P("rows", None, None, None), P("rows"))
    out_specs = (P("cols", "rows"), P(None, "cols"))
    return jax.shard_map(body, mesh=mesh, in_specs=in_specs, out_specs=out_specs, check_vma=False)
```

profile of v0, /device:TPU:0, one launch (start us, length us, event | category | flops | bytes accessed | tf_op | source)
XLA Modules:
  0.0 539.1 jit_solution(13265493274930220181)
XLA Ops:
  7.2 1.1 convert_element_type.16
  9.8 6.0 %collective-permute-start.1 = (bf16[16,1,256]{2,0,1:T(8,128)(2,1)S(1)}, bf16[16,1,256]{2,0,1:T(8,128)(2,1)S(1)}, u32[]{:S(2)}, u32[]{:S(2)}) collective-permute-start(bf16[16,1,256]{2,0,1:T(8,128)(2,1)S(1)} %get-tuple-element.23), channel_id=1, source_target_pairs={{4,0},{8,4},{12,8},{16,12},{20,16},{24,20},{28,24},{32,28},{36,32}... | collective-permute-start | bytes 24584 | tf_op jit(solution)/shard_map/ppermute | solution.py:18
  16.5 3.4 fusion.60
  19.9 3.6 fusion.84
  23.5 3.5 fusion.81
  27.0 39.3 %all-gather.7.cloned.1.call-done = bf16[16,1024,256]{2,0,1:T(8,128)(2,1)} async-done(((bf16[16,32,256]{2,0,1:T(8,128)(2,1)}), bf16[16,1024,256]{2,0,1:T(8,128)(2,1)}) %all-gather.7.cloned.1.call-update) | async-done | bytes 8388624 | tf_op jit(solution)/shard_map/all_gather | solution.py:42
  66.4 3.9 gather_fusion
  70.3 3.4 fusion.72
  75.4 2.8 collective-permute-start.3
  78.2 3.4 fusion.36
  81.6 3.6 fusion.16
  85.2 42.1 %all-gather.9.cloned.1.call-done = bf16[16,1024,256]{2,0,1:T(8,128)(2,1)} async-done(((bf16[16,32,256]{2,0,1:T(8,128)(2,1)}), bf16[16,1024,256]{2,0,1:T(8,128)(2,1)}) %all-gather.9.cloned.1.call-update) | async-done | bytes 8388624 | tf_op jit(solution)/shard_map/all_gather | solution.py:42
  127.3 3.9 gather_fusion.1
  131.2 3.4 fusion.6
  134.7 3.4 fusion.141
  139.7 2.8 collective-permute-start.5
  142.5 3.4 fusion.34
  145.9 3.6 fusion.14
  149.6 42.1 %all-gather.11.cloned.1.call-done = bf16[16,1024,256]{2,0,1:T(8,128)(2,1)} async-done(((bf16[16,32,256]{2,0,1:T(8,128)(2,1)}), bf16[16,1024,256]{2,0,1:T(8,128)(2,1)}) %all-gather.11.cloned.1.call-update) | async-done | bytes 8388624 | tf_op jit(solution)/shard_map/all_gather | solution.py:42
  191.6 3.9 gather_fusion.2
  195.6 3.4 fusion.4
  199.0 3.4 fusion.129
  202.5 0.7 copy.155
  204.0 2.8 collective-permute-start.7
  206.9 3.4 fusion.32
  210.3 3.6 fusion.12
  213.9 42.1 %all-gather.13.cloned.1.call-done = bf16[16,1024,256]{2,0,1:T(8,128)(2,1)} async-done(((bf16[16,32,256]{2,0,1:T(8,128)(2,1)}), bf16[16,1024,256]{2,0,1:T(8,128)(2,1)}) %all-gather.13.cloned.1.call-update) | async-done | bytes 8388624 | tf_op jit(solution)/shard_map/all_gather | solution.py:42
  256.0 3.9 gather_fusion.3
  259.9 3.4 fusion.2
  263.3 3.4 fusion.117
  266.8 0.9 fusion.230
  267.7 0.7 copy.154
  269.2 2.8 collective-permute-start.9
  272.0 3.4 fusion.30
  275.5 3.8 fusion.10
  279.3 18.8 %all-gather.15.cloned.1.call-done = f32[64,8192]{1,0:T(8,128)} async-done(((f32[16,8192]{1,0:T(8,128)}), f32[64,8192]{1,0:T(8,128)}) %all-gather.15.cloned.1.call-update) | async-done | bytes 2097168 | tf_op jit(solution)/shard_map/all_gather | solution.py:55
  298.1 3.3 fusion.239
  301.5 51.9 %all-gather.17.cloned.1.call-done = bf16[16,1024,256]{2,0,1:T(8,128)(2,1)} async-done(((bf16[16,32,256]{2,0,1:T(8,128)(2,1)}), bf16[16,1024,256]{2,0,1:T(8,128)(2,1)}) %all-gather.17.cloned.1.call-update) | async-done | bytes 8388624 | tf_op jit(solution)/shard_map/all_gather | solution.py:42
  353.3 3.9 gather_fusion.4
  357.3 3.4 fusion
  360.7 3.6 fusion.105
  364.4 1.7 fusion.240
  366.1 126.6 %all-reduce = (f32[64,16]{0,1:T(8,128)S(1)}, f32[64,16]{0,1:T(8,128)S(1)}) all-reduce(f32[64,16]{0,1:T(8,128)S(1)} %fusion.239, f32[64,16]{0,1:T(8,128)S(1)} %fusion.240), channel_id=1, replica_groups=mesh['rows'=32,'cols'=4] {'rows'}, use_global_device_ids=true, to_apply=%region_0.2 | all-reduce | flops 2048 | bytes 16384 | tf_op jit(solution)/shard_map/psum | solution.py:59
  492.6 12.4 %all_gather.29 = f32[64,64]{0,1:T(8,128)S(1)} all-gather(f32[64,16]{0,1:T(8,128)S(1)} %get-tuple-element.3), channel_id=1, replica_groups=mesh['rows'=32,'cols'=4] {'cols'}, dimensions={1}, use_global_device_ids=true | all-gather | bytes 20480 | tf_op jit(solution)/shard_map/all_gather | solution.py:60
  505.2 5.8 %cholesky.17 = f32[64,64]{1,0:T(8,128)S(1)} custom-call(f32[64,64]{1,0:T(8,128)S(1)} %fusion.202), custom_call_target="Cholesky" | custom-call | tf_op jit(solution)/shard_map/jit(cholesky)/cholesky | solution.py:65
  512.4 4.9 custom-call.6
  517.5 11.9 %all_gather.31 = f32[64,64]{0,1:T(8,128)S(1)} all-gather(f32[64,16]{0,1:T(8,128)S(1)} %get-tuple-element.4), channel_id=1, replica_groups=mesh['rows'=32,'cols'=4] {'cols'}, dimensions={1}, use_global_device_ids=true | all-gather | bytes 20480 | tf_op jit(solution)/shard_map/all_gather | solution.py:64
  530.4 1.9 fusion.206
  (71 shorter events, 10.0 us)
Async XLA Ops:
  7.2 59.2 %all-gather.7.cloned.1.call-start = ((), (), s32[]{:S(2)}) async-start(), calls=%async_computation | async-start | bytes 8650752 | tf_op jit(solution)/shard_map/all_gather | solution.py:42
  9.0 118.3 %all-gather.9.cloned.1.call-start = ((), (), s32[]{:S(2)}) async-start(), calls=%async_computation.1 | async-start | bytes 8650752 | tf_op jit(solution)/shard_map/all_gather | solution.py:42
  9.8 10.1 %collective-permute-start = (bf16[16,1,256]{2,0,1:T(8,128)(2,1)S(1)}, bf16[16,1,256]{2,0,1:T(8,128)(2,1)S(1)}, u32[]{:S(2)}, u32[]{:S(2)}) collective-permute-start(bf16[16,1,256]{2,0,1:T(8,128)(2,1)S(1)} %get-tuple-element.24), channel_id=1, source_target_pairs={{0,4},{4,8},{8,12},{12,16},{16,20},{20,24},{24,28},{28,32},{32,36}... | collective-permute-start | bytes 24584 | tf_op jit(solution)/shard_map/ppermute | solution.py:15
  9.8 13.7 %collective-permute-start.1 = (bf16[16,1,256]{2,0,1:T(8,128)(2,1)S(1)}, bf16[16,1,256]{2,0,1:T(8,128)(2,1)S(1)}, u32[]{:S(2)}, u32[]{:S(2)}) collective-permute-start(bf16[16,1,256]{2,0,1:T(8,128)(2,1)S(1)} %get-tuple-element.23), channel_id=1, source_target_pairs={{4,0},{8,4},{12,8},{16,12},{20,16},{24,20},{28,24},{32,28},{36,32}... | collective-permute-start | bytes 24584 | tf_op jit(solution)/shard_map/ppermute | solution.py:18
  19.9 3.6 copy-start.4
  23.5 50.3 %copy-start.2 = (f32[16,8192]{1,0:T(8,128)S(1)}, f32[16,8192]{1,0:T(8,128)}, u32[]{:S(2)}) copy-start(f32[16,8192]{1,0:T(8,128)} %param.5) | copy-start | bytes 1572868
  74.6 117.0 %all-gather.11.cloned.1.call-start = ((), (), s32[]{:S(2)}) async-start(), calls=%async_computation.2 | async-start | bytes 8650752 | tf_op jit(solution)/shard_map/all_gather | solution.py:42
  75.4 6.2 %collective-permute-start.3 = (bf16[16,1,256]{2,0,1:T(8,128)(2,1)S(1)}, bf16[16,1,256]{2,0,1:T(8,128)(2,1)S(1)}, u32[]{:S(2)}, u32[]{:S(2)}) collective-permute-start(bf16[16,1,256]{2,0,1:T(8,128)(2,1)S(1)} %get-tuple-element.22), channel_id=1, source_target_pairs={{4,0},{8,4},{12,8},{16,12},{20,16},{24,20},{28,24},{32,28},{36,32}... | collective-permute-start | bytes 24584 | tf_op jit(solution)/shard_map/ppermute | solution.py:18
  81.6 53.1 %copy-start.5 = (bf16[2,32,8,256]{3,2,0,1:T(8,128)(2,1)S(1)}, bf16[2,32,8,256]{3,2,0,1:T(8,128)(2,1)}, u32[]{:S(2)}) copy-start(bf16[2,32,8,256]{3,2,0,1:T(8,128)(2,1)} %copy.157) | copy-start | bytes 786436
  81.6 53.1 %collective-permute-start.2 = (bf16[16,1,256]{2,0,1:T(8,128)(2,1)S(1)}, bf16[16,1,256]{2,0,1:T(8,128)(2,1)S(1)}, u32[]{:S(2)}, u32[]{:S(2)}) collective-permute-start(bf16[16,1,256]{2,0,1:T(8,128)(2,1)S(1)} %get-tuple-element.21), channel_id=1, source_target_pairs={{0,4},{4,8},{8,12},{12,16},{16,20},{20,24},{24,28},{28,32},{32,36}... | collective-permute-start | bytes 24584 | tf_op jit(solution)/shard_map/ppermute | solution.py:15
  138.9 117.0 %all-gather.13.cloned.1.call-start = ((), (), s32[]{:S(2)}) async-start(), calls=%async_computation.3 | async-start | bytes 8650752 | tf_op jit(solution)/shard_map/all_gather | solution.py:42
  139.7 6.2 %collective-permute-start.5 = (bf16[16,1,256]{2,0,1:T(8,128)(2,1)S(1)}, bf16[16,1,256]{2,0,1:T(8,128)(2,1)S(1)}, u32[]{:S(2)}, u32[]{:S(2)}) collective-permute-start(bf16[16,1,256]{2,0,1:T(8,128)(2,1)S(1)} %get-tuple-element.20), channel_id=1, source_target_pairs={{4,0},{8,4},{12,8},{16,12},{20,16},{24,20},{28,24},{32,28},{36,32}... | collective-permute-start | bytes 24584 | tf_op jit(solution)/shard_map/ppermute | solution.py:18
  145.9 53.1 %copy-start.6 = (bf16[2,32,8,256]{3,2,0,1:T(8,128)(2,1)S(1)}, bf16[2,32,8,256]{3,2,0,1:T(8,128)(2,1)}, u32[]{:S(2)}) copy-start(bf16[2,32,8,256]{3,2,0,1:T(8,128)(2,1)} %copy.156) | copy-start | bytes 786436
  145.9 53.1 %collective-permute-start.4 = (bf16[16,1,256]{2,0,1:T(8,128)(2,1)S(1)}, bf16[16,1,256]{2,0,1:T(8,128)(2,1)S(1)}, u32[]{:S(2)}, u32[]{:S(2)}) collective-permute-start(bf16[16,1,256]{2,0,1:T(8,128)(2,1)S(1)} %get-tuple-element.19), channel_id=1, source_target_pairs={{0,4},{4,8},{8,12},{12,16},{16,20},{20,24},{24,28},{28,32},{32,36}... | collective-permute-start | bytes 24584 | tf_op jit(solution)/shard_map/ppermute | solution.py:15
  203.3 94.9 %all-gather.15.cloned.1.call-start = ((), (), s32[]{:S(2)}) async-start(), calls=%async_computation.4 | async-start | bytes 2621440 | tf_op jit(solution)/shard_map/all_gather | solution.py:55
  204.0 6.2 %collective-permute-start.7 = (bf16[16,1,256]{2,0,1:T(8,128)(2,1)S(1)}, bf16[16,1,256]{2,0,1:T(8,128)(2,1)S(1)}, u32[]{:S(2)}, u32[]{:S(2)}) collective-permute-start(bf16[16,1,256]{2,0,1:T(8,128)(2,1)S(1)} %get-tuple-element.18), channel_id=1, source_target_pairs={{4,0},{8,4},{12,8},{16,12},{20,16},{24,20},{28,24},{32,28},{36,32}... | collective-permute-start | bytes 24584 | tf_op jit(solution)/shard_map/ppermute | solution.py:18
  210.3 53.1 %copy-start.7 = (bf16[2,32,8,256]{3,2,0,1:T(8,128)(2,1)S(1)}, bf16[2,32,8,256]{3,2,0,1:T(8,128)(2,1)}, u32[]{:S(2)}) copy-start(bf16[2,32,8,256]{3,2,0,1:T(8,128)(2,1)} %copy.155) | copy-start | bytes 786436
  210.3 53.1 %collective-permute-start.6 = (bf16[16,1,256]{2,0,1:T(8,128)(2,1)S(1)}, bf16[16,1,256]{2,0,1:T(8,128)(2,1)S(1)}, u32[]{:S(2)}, u32[]{:S(2)}) collective-permute-start(bf16[16,1,256]{2,0,1:T(8,128)(2,1)S(1)} %get-tuple-element.17), channel_id=1, source_target_pairs={{0,4},{4,8},{8,12},{12,16},{16,20},{20,24},{24,28},{28,32},{32,36}... | collective-permute-start | bytes 24584 | tf_op jit(solution)/shard_map/ppermute | solution.py:15
  267.7 85.7 %all-gather.17.cloned.1.call-start = ((), (), s32[]{:S(2)}) async-start(), calls=%async_computation.5 | async-start | bytes 8650752 | tf_op jit(solution)/shard_map/all_gather | solution.py:42
  269.2 6.2 %collective-permute-start.9 = (bf16[16,1,256]{2,0,1:T(8,128)(2,1)S(1)}, bf16[16,1,256]{2,0,1:T(8,128)(2,1)S(1)}, u32[]{:S(2)}, u32[]{:S(2)}) collective-permute-start(bf16[16,1,256]{2,0,1:T(8,128)(2,1)S(1)} %get-tuple-element.16), channel_id=1, source_target_pairs={{4,0},{8,4},{12,8},{16,12},{20,16},{24,20},{28,24},{32,28},{36,32}... | collective-permute-start | bytes 24584 | tf_op jit(solution)/shard_map/ppermute | solution.py:18
  275.4 22.7 %copy-start.1 = (f32[16,8192]{1,0:T(8,128)S(1)}, f32[16,8192]{1,0:T(8,128)}, u32[]{:S(2)}) copy-start(f32[16,8192]{1,0:T(8,128)} %get-tuple-element.6) | copy-start | bytes 1572868
  275.4 85.3 %copy-start.3 = (bf16[2,32,8,256]{3,2,0,1:T(8,128)(2,1)S(1)}, bf16[2,32,8,256]{3,2,0,1:T(8,128)(2,1)}, u32[]{:S(2)}) copy-start(bf16[2,32,8,256]{3,2,0,1:T(8,128)(2,1)} %copy.154) | copy-start | bytes 786436
  275.4 85.3 %collective-permute-start.8 = (bf16[16,1,256]{2,0,1:T(8,128)(2,1)S(1)}, bf16[16,1,256]{2,0,1:T(8,128)(2,1)S(1)}, u32[]{:S(2)}, u32[]{:S(2)}) collective-permute-start(bf16[16,1,256]{2,0,1:T(8,128)(2,1)S(1)} %get-tuple-element.15), channel_id=1, source_target_pairs={{0,4},{4,8},{8,12},{12,16},{16,20},{20,24},{24,28},{28,32},{32,36}... | collective-permute-start | bytes 24584 | tf_op jit(solution)/shard_map/ppermute | solution.py:15
  360.7 3.6 copy-start
Sparse Core Ops, SparseCore 0:
  10.8 55.4 all-gather.6
  74.7 52.5 all-gather.8
  139.1 52.5 all-gather.10
  203.4 52.5 all-gather.12
  267.8 30.2 all-gather.14
  300.2 53.0 all-gather.16
where the time goes:
time: 540 us; the launch traced here: 539 us
  waiting for transfers between devices  236 us (44%)
  blocking collectives  151 us (28%)
  matrix products  77.1 us (14%)
  local copies, waits for them, and re-layouts  27.9 us (5%)
  starting transfers between devices  17.6 us (3%)
  other arithmetic  14.9 us (3%)
  between operations  14.4 us (3%)
    all_gather x5, waiting for transfers between devices, apply_generator(): piece = lax.all_gather(shaped, 'rows', axis=1, tiled=True)  217 us
    psum x1, blocking collectives, body(): gram_mine = lax.psum(gram_part, 'rows')  127 us
    dot_general x20, matrix products, block_product(): jnp.einsum('jbt,bst->jbs', pieces, blocks[:, position], preferred_element...  69.5 us
    gather x5, local copies, waits for them, and re-layouts, apply_generator(): taken = jnp.take(piece, jnp.clip(far_cols, 0, piece.shape[1] - 1), axis=1)  19.7 us
    all_gather x1, waiting for transfers between devices, body(): whole_iterate = lax.all_gather(iterate, 'cols', axis=0, tiled=True)  18.8 us
    ppermute x5, starting transfers between devices, with_halo(): lax.ppermute(lax.slice_in_dim(block, 0, width, axis=dim), axis, backward)  17.3 us
    all_gather x1, blocking collectives, body(): gram = lax.all_gather(gram_mine, 'cols', axis=1, tiled=True) / total_states  12.4 us
    all_gather x1, blocking collectives, body(): lax.all_gather(product_mine, 'cols', axis=1, tiled=True) / total_states  11.9 us
  transfers between devices with their start and end apart: 16, of which 6 were waited for; matrix products, arithmetic and copies ran while one was open for 14% of the time, Pallas kernels for 0%

commit v1 on v0

--- a/solution.py
+++ b/solution.py
@@ -52,7 +52,12 @@
     iterate = basis
     for step in range(ITERS):
         iterate = iterate + 0.2 * apply_generator(iterate.astype(jnp.bfloat16))
-    whole_iterate = lax.all_gather(iterate, "cols", axis=0, tiled=True)
+    ring = [iterate]
+    for hop in range(3):
+        ring.append(lax.ppermute(ring[-1], "cols", [(dev, (dev + 1) % 4) for dev in range(4)]))
+    whole_iterate = jnp.roll(
+        jnp.concatenate(ring[::-1], axis=0), (lax.axis_index("cols") + 1) * ring[0].shape[0], axis=0
+    )
     contract = (((1,), (1,)), ((), ()))
     gram_part = lax.dot_general(whole_iterate, iterate, contract, precision=highest)
     column_start = lax.axis_index("cols") * width

time: 540 us -> 509 us (0.943)
  waiting for transfers between devices: 236 us -> 203 us
    all_gather x5, waiting for transfers between devices: 217 us -> 171 us  [apply_generator(): piece = lax.all_gather(shaped, 'rows', axis=1, tiled=True)]
    ppermute x0 -> x3, waiting for transfers between devices: none -> 31.9 us  [body(): lax.ppermute(ring[-1], 'cols', [(dev, (dev + 1) % 4) for dev in range(4)])]
    all_gather x1 -> x0, waiting for transfers between devices: 18.8 us -> none  [body(): whole_iterate = lax.all_gather(iterate, 'cols', axis=0, tiled=True)]
  transfers between devices with their start and end apart: 16 -> 18, of which waited for: 6 -> 8; matrix products, arithmetic and copies ran while one was open for 14% -> 15% of each run, Pallas kernels for 0% -> 0%
where the time goes in v1:
time: 509 us; the launch traced here: 507 us
  waiting for transfers between devices  203 us (40%)
  blocking collectives  151 us (30%)
  matrix products  76.5 us (15%)
  local copies, waits for them, and re-layouts  30.1 us (6%)
  starting transfers between devices  18.3 us (4%)
  between operations  14.2 us (3%)
  other arithmetic  14.1 us (3%)
    all_gather x5, waiting for transfers between devices, apply_generator(): piece = lax.all_gather(shaped, 'rows', axis=1, tiled=True)  171 us
    psum x1, blocking collectives, body(): gram_mine = lax.psum(gram_part, 'rows')  127 us
    dot_general x20, matrix products, block_product(): jnp.einsum('jbt,bst->jbs', pieces, blocks[:, position], preferred_element...  68.9 us
    ppermute x3, waiting for transfers between devices, body(): lax.ppermute(ring[-1], 'cols', [(dev, (dev + 1) % 4) for dev in range(4)])  31.9 us
    gather x5, local copies, waits for them, and re-layouts, apply_generator(): taken = jnp.take(piece, jnp.clip(far_cols, 0, piece.shape[1] - 1), axis=1)  19.7 us
    ppermute x5, starting transfers between devices, with_halo(): lax.ppermute(lax.slice_in_dim(block, 0, width, axis=dim), axis, backward)  16.3 us
    all_gather x1, blocking collectives, body(): gram = lax.all_gather(gram_mine, 'cols', axis=1, tiled=True) / total_states  12.4 us
    all_gather x1, blocking collectives, body(): lax.all_gather(product_mine, 'cols', axis=1, tiled=True) / total_states  11.9 us
  transfers between devices with their start and end apart: 18, of which 8 were waited for; matrix products, arithmetic and copies ran while one was open for 15% of the time, Pallas kernels for 0%

profile of v1, /device:TPU:0, one launch (start us, length us, event | category | flops | bytes accessed | tf_op | source)
XLA Modules:
  0.0 507.3 jit_solution(8983625059101979984)
XLA Ops:
  9.8 6.0 %collective-permute-start.1 = (bf16[16,1,256]{2,0,1:T(8,128)(2,1)S(1)}, bf16[16,1,256]{2,0,1:T(8,128)(2,1)S(1)}, u32[]{:S(2)}, u32[]{:S(2)}) collective-permute-start(bf16[16,1,256]{2,0,1:T(8,128)(2,1)S(1)} %get-tuple-element.23), channel_id=1, source_target_pairs={{4,0},{8,4},{12,8},{16,12},{20,16},{24,20},{28,24},{32,28},{36,32}... | collective-permute-start | bytes 24584 | tf_op jit(solution)/shard_map/ppermute | solution.py:18
  16.5 3.4 fusion.66
  19.9 3.4 fusion.90
  23.3 3.5 fusion.87
  26.8 39.6 %all-gather.6.cloned.1.call-done = bf16[16,1024,256]{2,0,1:T(8,128)(2,1)} async-done(((bf16[16,32,256]{2,0,1:T(8,128)(2,1)}), bf16[16,1024,256]{2,0,1:T(8,128)(2,1)}) %all-gather.6.cloned.1.call-update) | async-done | bytes 8388624 | tf_op jit(solution)/shard_map/all_gather | solution.py:42
  66.4 3.9 gather_fusion
  70.3 3.4 fusion.78
  75.4 2.8 collective-permute-start.3
  78.2 3.4 fusion.36
  81.6 3.4 fusion.16
  85.0 42.2 %all-gather.8.cloned.1.call-done = bf16[16,1024,256]{2,0,1:T(8,128)(2,1)} async-done(((bf16[16,32,256]{2,0,1:T(8,128)(2,1)}), bf16[16,1024,256]{2,0,1:T(8,128)(2,1)}) %all-gather.8.cloned.1.call-update) | async-done | bytes 8388624 | tf_op jit(solution)/shard_map/all_gather | solution.py:42
  127.3 3.9 gather_fusion.1
  131.2 3.4 fusion.6
  134.6 3.4 fusion.147
  139.7 2.8 collective-permute-start.5
  142.5 3.4 fusion.34
  145.9 3.4 fusion.14
  149.4 42.2 %all-gather.10.cloned.1.call-done = bf16[16,1024,256]{2,0,1:T(8,128)(2,1)} async-done(((bf16[16,32,256]{2,0,1:T(8,128)(2,1)}), bf16[16,1024,256]{2,0,1:T(8,128)(2,1)}) %all-gather.10.cloned.1.call-update) | async-done | bytes 8388624 | tf_op jit(solution)/shard_map/all_gather | solution.py:42
  191.6 3.9 gather_fusion.2
  195.6 3.4 fusion.4
  199.0 3.4 fusion.135
  204.0 2.8 collective-permute-start.7
  206.8 3.4 fusion.32
  210.2 3.4 fusion.12
  213.7 42.2 %all-gather.12.cloned.1.call-done = bf16[16,1024,256]{2,0,1:T(8,128)(2,1)} async-done(((bf16[16,32,256]{2,0,1:T(8,128)(2,1)}), bf16[16,1024,256]{2,0,1:T(8,128)(2,1)}) %all-gather.12.cloned.1.call-update) | async-done | bytes 8388624 | tf_op jit(solution)/shard_map/all_gather | solution.py:42
  255.9 3.9 gather_fusion.3
  259.9 3.4 fusion.2
  263.3 3.4 fusion.123
  267.6 1.5 collective-permute-start.8
  269.1 13.8 %collective-permute-done.8 = f32[16,8192]{1,0:T(8,128)S(1)} collective-permute-done((f32[16,8192]{1,0:T(8,128)S(1)}, f32[16,8192]{1,0:T(8,128)S(1)}, u32[]{:S(2)}, u32[]{:S(2)}) %collective-permute-start.8) | collective-permute-done | bytes 524320 | tf_op jit(solution)/shard_map/ppermute | solution.py:57
  283.9 1.8 collective-permute-start.12
  285.8 3.4 fusion.30
  289.2 8.4 %collective-permute-done.9 = f32[16,8192]{1,0:T(8,128)S(1)} collective-permute-done((f32[16,8192]{1,0:T(8,128)S(1)}, f32[16,8192]{1,0:T(8,128)S(1)}, u32[]{:S(2)}, u32[]{:S(2)}) %collective-permute-start.9) | collective-permute-done | bytes 524320 | tf_op jit(solution)/shard_map/ppermute | solution.py:57
  297.6 4.0 fusion.10
  301.5 9.7 %collective-permute-done.10 = f32[16,8192]{1,0:T(8,128)S(1)} collective-permute-done((f32[16,8192]{1,0:T(8,128)S(1)}, f32[16,8192]{1,0:T(8,128)S(1)}, u32[]{:S(2)}, u32[]{:S(2)}) %collective-permute-start.10) | collective-permute-done | bytes 524320 | tf_op jit(solution)/shard_map/ppermute | solution.py:57
  311.6 2.0 copy-done
  313.6 1.7 fusion.64
  315.3 5.0 all-gather.14.cloned.1.call-done
  320.3 3.9 gather_fusion.4
  324.2 3.4 fusion
  327.6 3.5 fusion.111
  331.2 1.8 fusion.60
  333.0 126.6 %all-reduce = (f32[64,16]{0,1:T(8,128)S(1)}, f32[64,16]{0,1:T(8,128)S(1)}) all-reduce(f32[64,16]{0,1:T(8,128)S(1)} %fusion.64, f32[64,16]{0,1:T(8,128)S(1)} %fusion.60), channel_id=1, replica_groups=mesh['rows'=32,'cols'=4] {'rows'}, use_global_device_ids=true, to_apply=%region_0.2 | all-reduce | flops 2048 | bytes 16384 | tf_op jit(solution)/shard_map/psum | solution.py:64
  459.6 12.4 %all_gather.25 = f32[64,64]{0,1:T(8,128)S(1)} all-gather(f32[64,16]{0,1:T(8,128)S(1)} %get-tuple-element.3), channel_id=1, replica_groups=mesh['rows'=32,'cols'=4] {'cols'}, dimensions={1}, use_global_device_ids=true | all-gather | bytes 20480 | tf_op jit(solution)/shard_map/all_gather | solution.py:65
  472.1 5.8 %cholesky.17 = f32[64,64]{1,0:T(8,128)S(1)} custom-call(f32[64,64]{1,0:T(8,128)S(1)} %fusion.208), custom_call_target="Cholesky" | custom-call | tf_op jit(solution)/shard_map/jit(cholesky)/cholesky | solution.py:70
  479.3 4.9 custom-call.6
  484.4 11.9 %all_gather.27 = f32[64,64]{0,1:T(8,128)S(1)} all-gather(f32[64,16]{0,1:T(8,128)S(1)} %get-tuple-element.4), channel_id=1, replica_groups=mesh['rows'=32,'cols'=4] {'cols'}, dimensions={1}, use_global_device_ids=true | all-gather | bytes 20480 | tf_op jit(solution)/shard_map/all_gather | solution.py:69
  496.7 3.5 fusion.62
  (82 shorter events, 12.9 us)
Async XLA Ops:
  7.2 59.2 %all-gather.6.cloned.1.call-start = ((), (), s32[]{:S(2)}) async-start(), calls=%async_computation | async-start | bytes 8650752 | tf_op jit(solution)/shard_map/all_gather | solution.py:42
  9.0 10.9 %copy-start.4 = (bf16[2,32,8,256]{3,2,0,1:T(8,128)(2,1)S(1)}, bf16[2,32,8,256]{3,2,0,1:T(8,128)(2,1)}, u32[]{:S(2)}) copy-start(bf16[2,32,8,256]{3,2,0,1:T(8,128)(2,1)} %copy.158) | copy-start | bytes 786436
  9.0 118.3 %all-gather.8.cloned.1.call-start = ((), (), s32[]{:S(2)}) async-start(), calls=%async_computation.1 | async-start | bytes 8650752 | tf_op jit(solution)/shard_map/all_gather | solution.py:42
  9.8 10.1 %collective-permute-start = (bf16[16,1,256]{2,0,1:T(8,128)(2,1)S(1)}, bf16[16,1,256]{2,0,1:T(8,128)(2,1)S(1)}, u32[]{:S(2)}, u32[]{:S(2)}) collective-permute-start(bf16[16,1,256]{2,0,1:T(8,128)(2,1)S(1)} %get-tuple-element.24), channel_id=1, source_target_pairs={{0,4},{4,8},{8,12},{12,16},{16,20},{20,24},{24,28},{28,32},{32,36}... | collective-permute-start | bytes 24584 | tf_op jit(solution)/shard_map/ppermute | solution.py:15
  9.8 13.5 %collective-permute-start.1 = (bf16[16,1,256]{2,0,1:T(8,128)(2,1)S(1)}, bf16[16,1,256]{2,0,1:T(8,128)(2,1)S(1)}, u32[]{:S(2)}, u32[]{:S(2)}) collective-permute-start(bf16[16,1,256]{2,0,1:T(8,128)(2,1)S(1)} %get-tuple-element.23), channel_id=1, source_target_pairs={{4,0},{8,4},{12,8},{16,12},{20,16},{24,20},{28,24},{32,28},{36,32}... | collective-permute-start | bytes 24584 | tf_op jit(solution)/shard_map/ppermute | solution.py:18
  26.8 47.0 %copy-start.2 = (f32[16,8192]{1,0:T(8,128)S(1)}, f32[16,8192]{1,0:T(8,128)}, u32[]{:S(2)}) copy-start(f32[16,8192]{1,0:T(8,128)} %param.5) | copy-start | bytes 1572868
  74.6 7.0 %copy-start.5 = (bf16[2,32,8,256]{3,2,0,1:T(8,128)(2,1)S(1)}, bf16[2,32,8,256]{3,2,0,1:T(8,128)(2,1)}, u32[]{:S(2)}) copy-start(bf16[2,32,8,256]{3,2,0,1:T(8,128)(2,1)} %copy.157) | copy-start | bytes 786436
  74.6 117.0 %all-gather.10.cloned.1.call-start = ((), (), s32[]{:S(2)}) async-start(), calls=%async_computation.2 | async-start | bytes 8650752 | tf_op jit(solution)/shard_map/all_gather | solution.py:42
  75.4 6.2 %collective-permute-start.3 = (bf16[16,1,256]{2,0,1:T(8,128)(2,1)S(1)}, bf16[16,1,256]{2,0,1:T(8,128)(2,1)S(1)}, u32[]{:S(2)}, u32[]{:S(2)}) collective-permute-start(bf16[16,1,256]{2,0,1:T(8,128)(2,1)S(1)} %get-tuple-element.22), channel_id=1, source_target_pairs={{4,0},{8,4},{12,8},{16,12},{20,16},{24,20},{28,24},{32,28},{36,32}... | collective-permute-start | bytes 24584 | tf_op jit(solution)/shard_map/ppermute | solution.py:18
  81.6 53.1 %collective-permute-start.2 = (bf16[16,1,256]{2,0,1:T(8,128)(2,1)S(1)}, bf16[16,1,256]{2,0,1:T(8,128)(2,1)S(1)}, u32[]{:S(2)}, u32[]{:S(2)}) collective-permute-start(bf16[16,1,256]{2,0,1:T(8,128)(2,1)S(1)} %get-tuple-element.21), channel_id=1, source_target_pairs={{0,4},{4,8},{8,12},{12,16},{16,20},{20,24},{24,28},{28,32},{32,36}... | collective-permute-start | bytes 24584 | tf_op jit(solution)/shard_map/ppermute | solution.py:15
  138.9 7.0 %copy-start.6 = (bf16[2,32,8,256]{3,2,0,1:T(8,128)(2,1)S(1)}, bf16[2,32,8,256]{3,2,0,1:T(8,128)(2,1)}, u32[]{:S(2)}) copy-start(bf16[2,32,8,256]{3,2,0,1:T(8,128)(2,1)} %copy.156) | copy-start | bytes 786436
  138.9 117.0 %all-gather.12.cloned.1.call-start = ((), (), s32[]{:S(2)}) async-start(), calls=%async_computation.3 | async-start | bytes 8650752 | tf_op jit(solution)/shard_map/all_gather | solution.py:42
  139.7 6.2 %collective-permute-start.5 = (bf16[16,1,256]{2,0,1:T(8,128)(2,1)S(1)}, bf16[16,1,256]{2,0,1:T(8,128)(2,1)S(1)}, u32[]{:S(2)}, u32[]{:S(2)}) collective-permute-start(bf16[16,1,256]{2,0,1:T(8,128)(2,1)S(1)} %get-tuple-element.20), channel_id=1, source_target_pairs={{4,0},{8,4},{12,8},{16,12},{20,16},{24,20},{28,24},{32,28},{36,32}... | collective-permute-start | bytes 24584 | tf_op jit(solution)/shard_map/ppermute | solution.py:18
  145.9 53.1 %collective-permute-start.4 = (bf16[16,1,256]{2,0,1:T(8,128)(2,1)S(1)}, bf16[16,1,256]{2,0,1:T(8,128)(2,1)S(1)}, u32[]{:S(2)}, u32[]{:S(2)}) collective-permute-start(bf16[16,1,256]{2,0,1:T(8,128)(2,1)S(1)} %get-tuple-element.19), channel_id=1, source_target_pairs={{0,4},{4,8},{8,12},{12,16},{16,20},{20,24},{24,28},{28,32},{32,36}... | collective-permute-start | bytes 24584 | tf_op jit(solution)/shard_map/ppermute | solution.py:15
  203.2 7.0 %copy-start.7 = (bf16[2,32,8,256]{3,2,0,1:T(8,128)(2,1)S(1)}, bf16[2,32,8,256]{3,2,0,1:T(8,128)(2,1)}, u32[]{:S(2)}) copy-start(bf16[2,32,8,256]{3,2,0,1:T(8,128)(2,1)} %copy.155) | copy-start | bytes 786436
  203.3 117.0 %all-gather.14.cloned.1.call-start = ((), (), s32[]{:S(2)}) async-start(), calls=%async_computation.4 | async-start | bytes 8650752 | tf_op jit(solution)/shard_map/all_gather | solution.py:42
  204.0 6.2 %collective-permute-start.7 = (bf16[16,1,256]{2,0,1:T(8,128)(2,1)S(1)}, bf16[16,1,256]{2,0,1:T(8,128)(2,1)S(1)}, u32[]{:S(2)}, u32[]{:S(2)}) collective-permute-start(bf16[16,1,256]{2,0,1:T(8,128)(2,1)S(1)} %get-tuple-element.18), channel_id=1, source_target_pairs={{4,0},{8,4},{12,8},{16,12},{20,16},{24,20},{28,24},{32,28},{36,32}... | collective-permute-start | bytes 24584 | tf_op jit(solution)/shard_map/ppermute | solution.py:18
  210.2 53.1 %collective-permute-start.6 = (bf16[16,1,256]{2,0,1:T(8,128)(2,1)S(1)}, bf16[16,1,256]{2,0,1:T(8,128)(2,1)S(1)}, u32[]{:S(2)}, u32[]{:S(2)}) collective-permute-start(bf16[16,1,256]{2,0,1:T(8,128)(2,1)S(1)} %get-tuple-element.17), channel_id=1, source_target_pairs={{0,4},{4,8},{8,12},{12,16},{16,20},{20,24},{24,28},{28,32},{32,36}... | collective-permute-start | bytes 24584 | tf_op jit(solution)/shard_map/ppermute | solution.py:15
  267.5 30.0 %copy-start.3 = (bf16[2,32,8,256]{3,2,0,1:T(8,128)(2,1)S(1)}, bf16[2,32,8,256]{3,2,0,1:T(8,128)(2,1)}, u32[]{:S(2)}) copy-start(bf16[2,32,8,256]{3,2,0,1:T(8,128)(2,1)} %copy.154) | copy-start | bytes 786436
  267.6 15.4 %collective-permute-start.8 = (f32[16,8192]{1,0:T(8,128)S(1)}, f32[16,8192]{1,0:T(8,128)S(1)}, u32[]{:S(2)}, u32[]{:S(2)}) collective-permute-start(f32[16,8192]{1,0:T(8,128)S(1)} %get-tuple-element.6), channel_id=1, source_target_pairs={{0,1},{1,2},{2,3},{3,0},{4,5},{5,6},{6,7},{7,4},{8,9},{9,10},{10,1... | collective-permute-start | bytes 1572872 | tf_op jit(solution)/shard_map/ppermute | solution.py:57
  282.9 14.6 %collective-permute-start.9 = (f32[16,8192]{1,0:T(8,128)S(1)}, f32[16,8192]{1,0:T(8,128)S(1)}, u32[]{:S(2)}, u32[]{:S(2)}) collective-permute-start(f32[16,8192]{1,0:T(8,128)S(1)} %collective-permute-done.8), channel_id=1, source_target_pairs={{0,1},{1,2},{2,3},{3,0},{4,5},{5,6},{6,7},{7,4},{8,9},{9,10},{10,1... | collective-permute-start | bytes 1572872 | tf_op jit(solution)/shard_map/ppermute | solution.py:57
  283.9 13.6 %collective-permute-start.12 = (bf16[16,1,256]{2,0,1:T(8,128)(2,1)S(1)}, bf16[16,1,256]{2,0,1:T(8,128)(2,1)S(1)}, u32[]{:S(2)}, u32[]{:S(2)}) collective-permute-start(bf16[16,1,256]{2,0,1:T(8,128)(2,1)S(1)} %get-tuple-element.16), channel_id=1, source_target_pairs={{4,0},{8,4},{12,8},{16,12},{20,16},{24,20},{28,24},{32,28},{36,32}... | collective-permute-start | bytes 24584 | tf_op jit(solution)/shard_map/ppermute | solution.py:18
  289.2 38.5 %collective-permute-start.11 = (bf16[16,1,256]{2,0,1:T(8,128)(2,1)S(1)}, bf16[16,1,256]{2,0,1:T(8,128)(2,1)S(1)}, u32[]{:S(2)}, u32[]{:S(2)}) collective-permute-start(bf16[16,1,256]{2,0,1:T(8,128)(2,1)S(1)} %get-tuple-element.15), channel_id=1, source_target_pairs={{0,4},{4,8},{8,12},{12,16},{16,20},{20,24},{24,28},{28,32},{32,36}... | collective-permute-start | bytes 24584 | tf_op jit(solution)/shard_map/ppermute | solution.py:15
  297.5 13.7 %collective-permute-start.10 = (f32[16,8192]{1,0:T(8,128)S(1)}, f32[16,8192]{1,0:T(8,128)S(1)}, u32[]{:S(2)}, u32[]{:S(2)}) collective-permute-start(f32[16,8192]{1,0:T(8,128)S(1)} %collective-permute-done.9), channel_id=1, source_target_pairs={{0,1},{1,2},{2,3},{3,0},{4,5},{5,6},{6,7},{7,4},{8,9},{9,10},{10,1... | collective-permute-start | bytes 1572872 | tf_op jit(solution)/shard_map/ppermute | solution.py:57
  311.6 2.0 copy-start
  327.6 3.6 copy-start.1
Sparse Core Ops, SparseCore 0:
  10.8 55.4 all-gather.5
  74.7 52.5 all-gather.7
  139.0 52.5 all-gather.9
  203.4 52.5 all-gather.11
  267.7 52.5 all-gather.13
